TPU v7x, 32 devices: a whole 2x2x4 slice. The times are simulated.
32 devices in a mesh: client: 16 (over z, y, x), param: 2 (over core).
Axes of the slice: x: 2, y: 2, z: 4, core: 2. Of those that a mesh axis runs over, the one named last changes fastest.
Arguments:
- updates: float32 [32, 128, 3584], P('client', None, 'param'), as said below
- sample_counts: int32 [32], P('client'), may hold values from 16 to 1023
Outputs:
- median: float32 [128, 3584], P('client', 'param')
- shares: float32 [32], P('client')
Inputs may be any that keep to these rules, and one draw needn't show every extreme that they name: `updates`: each client's update is real-valued with every entry nonzero in general.
All inputs are finite; a program needn't handle non-finite values.
Results may differ from a plain program's by a relative error of at most 0.0001.
Values sent between devices are 32-bit elements; how exact they have to be, the bound alone decides.
A program may use at most 64 MiB of HBM per device.

v0:
```python
import jax
import jax.numpy as jnp
from jax import lax
from jax.sharding import PartitionSpec as P

ITERS = 2


smoothing = 1e-06


def weighted_sum(weights, updates):
    return jnp.einsum("c,crk->rk", weights, updates, precision=lax.Precision.HIGHEST)


def local(updates, sample_counts):
    local_clients = updates.shape[0]
    clients = local_clients * lax.axis_size("client")
    exchanged = lax.all_to_all(updates, "client", split_axis=1, concat_axis=0, tiled=True)
    counts_f = lax.all_gather(sample_counts, "client", axis=0, tiled=True).astype(jnp.float32)
    weights = counts_f
    for iteration in range(ITERS + 1):
        weight_sum = jnp.sum(weights)
        median = weighted_sum(weights, exchanged) / weight_sum
        if iteration < ITERS:
            distance_sq = jnp.sum((exchanged - median[None]) ** 2, axis=(1, 2))
            distance_sq = lax.psum(distance_sq, ("client", "param"))
            weights = counts_f / jnp.sqrt(distance_sq + smoothing)
    offset = lax.axis_index("client") * local_clients
    shares = lax.dynamic_slice_in_dim(clients * weights / weight_sum, offset, local_clients, 0)
    return (median, shares)


def solution(mesh):
    return jax.shard_map(
        local,
        mesh=mesh,
        in_specs=(P("client", None, "param"), P("client")),
        out_specs=(P("client", "param"), P("client")),
        check_vma=False,
    )
```

profile of v0, /device:TPU:0, one launch (start us, length us, event | category | flops | bytes accessed | tf_op | source)
XLA Modules:
  0.0 151.9 jit_solution(10207330861377633451)
XLA Ops:
  0.6 4.2 %copy.5 = f32[2,128,1792]{2,0,1:T(2,128)} copy(f32[2,128,1792]{2,1,0:T(8,128)} %param.2) | data formatting | bytes 3670016 | tf_op args[0]
  4.8 0.0 copy-start.2
  4.8 0.0 copy-start.1
  4.8 8.4 %all-to-all-start = ((f32[2,128,1792]{2,0,1:T(2,128)}), f32[2,128,1792]{2,0,1:T(2,128)S(1)}, u32[]{:S(2)}, u32[]{:S(2)}) async-start(f32[2,128,1792]{2,0,1:T(2,128)} %copy.5), calls=%async_computation | async-start | bytes 3670016 | tf_op jit(solution)/shard_map/all_to_all | solution.py:19
  13.3 0.0 copy-done.2
  13.3 0.6 dynamic-slice
  14.5 0.0 copy-done.1
  14.5 0.2 dynamic-update-slice
  14.8 41.2 %all-reduce = s32[32]{0:T(128)S(1)} all-reduce(s32[32]{0:T(128)S(1)} %dynamic-update-slice), channel_id=1, replica_groups=mesh['client'=16,'param'=2] {'client'}, use_global_device_ids=true, to_apply=%add | all-reduce | flops 32 | bytes 256
  56.0 0.6 convert_reduce_fusion
  56.6 0.0 all-to-all-done
  56.6 0.1 copy.28
  56.7 0.2 copy.7
  56.9 0.0 copy-start
  56.9 1.2 copy-done
  58.2 1.5 fusion.4
  59.7 0.7 bitcast_divide_fusion.2
  60.3 0.3 multiply_reduce_fusion.1
  60.7 0.1 copy.8
  60.7 0.1 reduce_sum.51
  60.8 39.6 %psum.14 = f32[32]{0:T(128)S(1)} all-reduce(f32[32]{0:T(128)S(1)} %reduce_sum.51), channel_id=1, replica_groups=mesh['client'=16,'param'=2] {'client','param'}, use_global_device_ids=true, to_apply=%region_2.0 | all-reduce | flops 32 | bytes 256 | tf_op jit(solution)/shard_map/psum | solution.py:27
  100.4 3.0 %fusion.2 = f32[1,8,1792]{2,0,1:T(1,128)S(1)} fusion(f32[32,8,1792]{2,1,0:T(8,128)} %bitcast.27, f32[32]{0:T(128)S(1)} %psum.14, s32[32]{0:T(128)S(1)} %all-reduce), kind=kOutput, calls=%fused_computation.5 | convolution fusion | flops 5505120 | bytes 1892608 | tf_op jit(solution)/shard_map/c,crk->rk/dot_general | solution.py:13
  103.4 0.6 fusion.10
  104.0 0.7 bitcast_divide_fusion.1
  104.7 0.3 multiply_reduce_fusion
  105.0 0.1 copy.9
  105.1 0.1 reduce_sum.54
  105.2 40.7 %psum.15 = f32[32]{0:T(128)S(1)} all-reduce(f32[32]{0:T(128)S(1)} %reduce_sum.54), channel_id=1, replica_groups=mesh['client'=16,'param'=2] {'client','param'}, use_global_device_ids=true, to_apply=%region_5.0 | all-reduce | flops 32 | bytes 256 | tf_op jit(solution)/shard_map/psum | solution.py:27
  145.9 3.0 %fusion = f32[1,8,1792]{2,0,1:T(1,128)S(1)} fusion(f32[32,8,1792]{2,1,0:T(8,128)} %bitcast.28, f32[32]{0:T(128)S(1)} %psum.15, s32[32]{0:T(128)S(1)} %all-reduce), kind=kOutput, calls=%fused_computation.3 | convolution fusion | flops 5505120 | bytes 1892608 | tf_op jit(solution)/shard_map/c,crk->rk/dot_general | solution.py:13
  148.8 0.6 fusion.11
  149.4 0.7 multiply_divide_fusion
  150.1 1.3 bitcast_divide_fusion
  151.4 0.6 dynamic_slice.3
  (1 shorter events, 0.0 us)
Async XLA Ops:
  4.8 8.5 %copy-start.2 = (u32[32]{0:T(128)S(1)}, u32[32]{0:T(128)}, u32[]{:S(2)}) copy-start(u32[32]{0:T(128)} %constant.22) | copy-start | bytes 388
  4.8 9.7 %copy-start.1 = (s32[2]{0:T(128)S(1)}, s32[2]{0:T(128)}, u32[]{:S(2)}) copy-start(s32[2]{0:T(128)} %param.3) | copy-start | bytes 28
  4.8 51.8 %all-to-all-start = ((f32[2,128,1792]{2,0,1:T(2,128)}), f32[2,128,1792]{2,0,1:T(2,128)S(1)}, u32[]{:S(2)}, u32[]{:S(2)}) async-start(f32[2,128,1792]{2,0,1:T(2,128)} %copy.5), calls=%async_computation | async-start | bytes 3670016 | tf_op jit(solution)/shard_map/all_to_all | solution.py:19
  56.9 1.3 copy-start
where the time goes:
time: 153 us; the launch traced here: 152 us
  blocking collectives  122 us (80%)
  starting transfers between devices  8.44 us (6%)
  local copies, waits for them, and re-layouts  7.48 us (5%)
  matrix products  7.39 us (5%)
  other arithmetic  5.7 us (4%)
    psum x2, blocking collectives, local(): distance_sq = lax.psum(distance_sq, ('client', 'param'))  80.3 us
    unnamed x1, blocking collectives  41.2 us
    all_to_all x1, starting transfers between devices, local(): lax.all_to_all(updates, 'client', split_axis=1, concat_axis=0, tiled=True)  8.44 us
    dot_general x3, matrix products, weighted_sum(): jnp.einsum('c,crk->rk', weights, updates, precision=lax.Precision.HIGHEST)  7.39 us
    unnamed x10, local copies, waits for them, and re-layouts  6.25 us
  transfers between devices with their start and end apart: 1, of which 0 were waited for; matrix products, arithmetic and copies ran while one was open for 1% of the time, Pallas kernels for 0%

commit v1 on v0

--- a/solution.py
+++ b/solution.py
@@ -1,10 +1,17 @@
+import functools
+
 import jax
 import jax.numpy as jnp
 from jax import lax
+from jax.experimental import pallas as pl
+from jax.experimental.pallas import tpu as pltpu
 from jax.sharding import PartitionSpec as P
 
 ITERS = 2
-
+LANES = 128
+SUBLANES = 8
+GROUPS = 2
+CHUNKS = 2
 
 smoothing = 1e-06
 
@@ -13,7 +20,7 @@
     return jnp.einsum("c,crk->rk", weights, updates, precision=lax.Precision.HIGHEST)
 
 
-def local(updates, sample_counts):
+def local_plain(updates, sample_counts):
     local_clients = updates.shape[0]
     clients = local_clients * lax.axis_size("client")
     exchanged = lax.all_to_all(updates, "client", split_axis=1, concat_axis=0, tiled=True)
@@ -31,6 +38,258 @@
     return (median, shares)
 
 
+def kernel(groups, members, cores, chunks, u_ref, cnt_ref, med_ref, share_ref,
+           held, cnt_send, cnt_held, dist_send, dist_held, dist_rows, weight, part, part_in, last, last_in,
+           own_sem, u_send, u_recv, c_send, c_recv, p_send, p_recv, l_send, l_recv, d_send, d_recv):
+    nc, cols = u_ref.shape[0], u_ref.shape[-1]
+    clients = nc * members
+    me, core = lax.axis_index("client"), lax.axis_index("param")
+    j, h = lax.rem(me, members), lax.div(me, members)
+    partner = lax.rem(me + members, groups * members)
+    rank = core * members + j
+    width = cols // chunks
+
+    def member(o, c):
+        return {"client": h * members + lax.rem(j + o, members), "param": lax.rem(core + c, cores)}
+
+    others = [(o, c) for c in range(cores) for o in range(members) if o or c]
+    barrier = pltpu.get_barrier_semaphore()
+    for o, c in others:
+        pl.semaphore_signal(barrier, inc=1, device_id=member(o, c), device_id_type=pl.DeviceIdType.MESH)
+    if groups > 1:
+        pl.semaphore_signal(barrier, inc=1, device_id={"client": partner}, device_id_type=pl.DeviceIdType.MESH)
+    own = []
+    for k in range(chunks):
+        sl = pl.ds(k * width, width)
+        own.append(pltpu.make_async_copy(u_ref.at[:, :, j, :, sl], held.at[j, :, :, :, sl], own_sem.at[k]))
+        own[-1].start()
+    for c in range(nc):
+        row = jnp.full((1, LANES), cnt_ref[c], jnp.int32).astype(jnp.float32)
+        cnt_send[c:c + 1, :] = row
+        cnt_held[j, c:c + 1, :] = row
+    pl.semaphore_wait(barrier, len(others) + (groups > 1))
+
+    def count_copy(o, slot):
+        return pltpu.make_async_remote_copy(
+            src_ref=cnt_send, dst_ref=cnt_held.at[slot], send_sem=c_send.at[o], recv_sem=c_recv.at[o],
+            device_id={"client": h * members + lax.rem(j + o, members)}, device_id_type=pl.DeviceIdType.MESH)
+
+    def rows_copy(o, k, slot):
+        to = lax.rem(j + o, members)
+        sl = pl.ds(k * width, width)
+        return pltpu.make_async_remote_copy(
+            src_ref=u_ref.at[:, :, to, :, sl], dst_ref=held.at[slot, :, :, :, sl],
+            send_sem=u_send.at[o, k], recv_sem=u_recv.at[o, k],
+            device_id={"client": h * members + to}, device_id_type=pl.DeviceIdType.MESH)
+
+    def source(o):
+        return lax.rem(j + members - o, members)
+
+    for o in range(1, members):
+        count_copy(o, j).start()
+    for k in range(chunks):
+        for o in range(1, members):
+            rows_copy(o, k, j).start()
+
+    def part_copy(i, k):
+        sl = pl.ds(k * width, width + (LANES if k == chunks - 1 else 0))
+        return pltpu.make_async_remote_copy(
+            src_ref=part.at[i, :, :, sl], dst_ref=part_in.at[i, :, :, sl],
+            send_sem=p_send.at[i, k], recv_sem=p_recv.at[i, k],
+            device_id={"client": partner}, device_id_type=pl.DeviceIdType.MESH)
+
+    def weights_now():
+        w = [jnp.broadcast_to(weight[c:c + 1, :], (SUBLANES, LANES)) for c in range(clients)]
+        total = w[0]
+        for x in w[1:]:
+            total = total + x
+        return w, total
+
+    def tile(t):
+        return pl.ds(pl.multiple_of(t * LANES, LANES), LANES)
+
+    def sum_tile(w, r, t):
+        acc = w[0] * held[0, 0, r, :, tile(t)]
+        for c in range(1, clients):
+            acc = acc + w[c] * held[c // nc, c % nc, r, :, tile(t)]
+        return acc
+
+    def send_part(i):
+        w, total = weights_now()
+        for r in range(groups):
+            part[i, r, :, pl.ds(cols, LANES)] = total
+        for k in range(chunks):
+            if i == 0:
+                own[k].wait()
+                for o in range(1, members):
+                    rows_copy(o, k, source(o)).wait_recv()
+
+            def body(t, carry):
+                for r in range(groups):
+                    part[i, r, :, tile(t)] = sum_tile(w, r, t)
+                return carry
+
+            lax.fori_loop(k * width // LANES, (k + 1) * width // LANES, body, 0)
+            if groups > 1:
+                part_copy(i, k).start()
+
+    def distances(i):
+        total = part[i, 0, :, pl.ds(cols, LANES)]
+        acc = tuple(jnp.zeros((SUBLANES, LANES), jnp.float32) for _ in range(clients))
+        if groups > 1:
+            part_copy(i, chunks - 1).wait_recv()
+            total = total + part_in[i, 0, :, pl.ds(cols, LANES)]
+        inverse = 1.0 / total
+        for k in range(chunks):
+            if groups > 1 and k < chunks - 1:
+                part_copy(i, k).wait_recv()
+
+            def body(t, acc):
+                acc = list(acc)
+                for r in range(groups):
+                    m = part[i, r, :, tile(t)]
+                    if groups > 1:
+                        m = m + part_in[i, r, :, tile(t)]
+                    m = m * inverse
+                    for c in range(clients):
+                        d = held[c // nc, c % nc, r, :, tile(t)] - m
+                        acc[c] = acc[c] + d * d
+                return tuple(acc)
+
+            acc = lax.fori_loop(k * width // LANES, (k + 1) * width // LANES, body, acc)
+        for c in range(clients):
+            dist_rows[c:c + 1, :] = jnp.sum(acc[c], axis=0, keepdims=True)
+        eye = (lax.broadcasted_iota(jnp.int32, (clients, LANES), 0)
+               == lax.broadcasted_iota(jnp.int32, (clients, LANES), 1))
+        column = jnp.sum(dist_rows[...], axis=1, keepdims=True)
+        row = jnp.sum(jnp.where(eye, column, 0.0), axis=0, keepdims=True)
+        dist_send[i] = row
+        dist_held[i, rank] = row
+
+        def copy(n, o, c, slot):
+            return pltpu.make_async_remote_copy(
+                src_ref=dist_send.at[i], dst_ref=dist_held.at[i, slot],
+                send_sem=d_send.at[i, n], recv_sem=d_recv.at[i, n],
+                device_id=member(o, c), device_id_type=pl.DeviceIdType.MESH)
+
+        for n, (o, c) in enumerate(others):
+            copy(n, o, c, rank).start()
+        for n, (o, c) in enumerate(others):
+            copy(n, o, c, lax.rem(core + cores - c, cores) * members + source(o)).wait_recv()
+        row = dist_held[i, 0]
+        for s in range(1, cores * members):
+            row = row + dist_held[i, s]
+        column = jnp.sum(jnp.where(eye, jnp.broadcast_to(row, eye.shape), 0.0), axis=1, keepdims=True)
+        root = jnp.sqrt(jnp.broadcast_to(column, eye.shape) + smoothing)
+        for c in range(clients):
+            weight[c:c + 1, :] = cnt_held[c // nc, c % nc:c % nc + 1, :] / root[c:c + 1, :]
+        for n, (o, c) in enumerate(others):
+            copy(n, o, c, rank).wait_send()
+
+    for o in range(1, members):
+        count_copy(o, source(o)).wait_recv()
+    for c in range(clients):
+        weight[c:c + 1, :] = cnt_held[c // nc, c % nc:c % nc + 1, :]
+    for i in range(ITERS):
+        send_part(i)
+        distances(i)
+
+    w, total = weights_now()
+    final = pltpu.make_async_remote_copy(
+        src_ref=last, dst_ref=last_in, send_sem=l_send, recv_sem=l_recv,
+        device_id={"client": partner}, device_id_type=pl.DeviceIdType.MESH)
+    if groups > 1:
+        last[:, pl.ds(cols, LANES)] = total
+
+        def body(t, carry):
+            last[:, tile(t)] = sum_tile(w, 1 - h, t)
+            return carry
+
+        lax.fori_loop(0, cols // LANES, body, 0)
+        final.start()
+
+    def body(t, carry):
+        med_ref[:, tile(t)] = sum_tile(w, h, t)
+        return carry
+
+    lax.fori_loop(0, cols // LANES, body, 0)
+    if groups > 1:
+        final.wait_recv()
+        total = total + last_in[:, pl.ds(cols, LANES)]
+    inverse = 1.0 / total
+
+    def body(t, carry):
+        m = med_ref[:, tile(t)]
+        if groups > 1:
+            m = m + last_in[:, tile(t)]
+        med_ref[:, tile(t)] = m * inverse
+        return carry
+
+    lax.fori_loop(0, cols // LANES, body, 0)
+    for c in range(nc):
+        share = (groups * clients) * weight[pl.ds(nc * j + c, 1), :] * inverse[0:1, :]
+        share_ref[c] = share[0, 0]
+
+    for o in range(1, members):
+        count_copy(o, j).wait_send()
+        for k in range(chunks):
+            rows_copy(o, k, j).wait_send()
+    if groups > 1:
+        for i in range(ITERS):
+            for k in range(chunks):
+                part_copy(i, k).wait_send()
+        final.wait_send()
+
+
+def local(updates, sample_counts):
+    nc, rows, cols = updates.shape
+    devices, cores = lax.axis_size("client"), lax.axis_size("param")
+    groups = GROUPS if devices % GROUPS == 0 and devices > GROUPS else 1
+    members = devices // groups
+    chunks = CHUNKS if cols % (CHUNKS * LANES) == 0 else 1
+    mine = rows // devices
+    if rows % devices or mine != SUBLANES or cols % LANES or members < 2 or nc * members > LANES:
+        return local_plain(updates, sample_counts)
+    clients = nc * members
+    f32 = jnp.float32
+    dma = pltpu.SemaphoreType.DMA
+    wide = cols + LANES
+    return pl.pallas_call(
+        functools.partial(kernel, groups, members, cores, chunks),
+        out_shape=(jax.ShapeDtypeStruct((mine, cols), f32), jax.ShapeDtypeStruct((nc,), f32)),
+        in_specs=[pl.BlockSpec(memory_space=pl.ANY), pl.BlockSpec(memory_space=pltpu.SMEM)],
+        out_specs=(pl.BlockSpec(memory_space=pltpu.VMEM), pl.BlockSpec(memory_space=pltpu.SMEM)),
+        scratch_shapes=[
+            pltpu.VMEM((members, nc, groups, mine, cols), f32),
+            pltpu.VMEM((nc, LANES), f32),
+            pltpu.VMEM((members, nc, LANES), f32),
+            pltpu.VMEM((ITERS, 1, LANES), f32),
+            pltpu.VMEM((ITERS, cores * members, 1, LANES), f32),
+            pltpu.VMEM((clients, LANES), f32),
+            pltpu.VMEM((clients, LANES), f32),
+            pltpu.VMEM((ITERS, groups, mine, wide), f32),
+            pltpu.VMEM((ITERS, groups, mine, wide), f32),
+            pltpu.VMEM((mine, wide), f32),
+            pltpu.VMEM((mine, wide), f32),
+            dma((chunks,)),
+            dma((members, chunks)),
+            dma((members, chunks)),
+            dma((members,)),
+            dma((members,)),
+            dma((ITERS, chunks)),
+            dma((ITERS, chunks)),
+            dma,
+            dma,
+            dma((ITERS, cores * members)),
+            dma((ITERS, cores * members)),
+        ],
+        compiler_params=pltpu.CompilerParams(
+            collective_id=0, has_side_effects=True, vmem_limit_bytes=32 * 1024 * 1024),
+        cost_estimate=pl.CostEstimate(
+            flops=16 * clients * groups * mine * cols, bytes_accessed=8 * nc * rows * cols, transcendentals=0),
+    )(updates.reshape(nc, groups, members, mine, cols), sample_counts)
+
+
 def solution(mesh):
     return jax.shard_map(
         local,

time: 153 us -> 63.4 us (0.41)
  blocking collectives: 122 us -> 0 us
  Pallas kernels: 0 us -> 59.3 us
  starting transfers between devices: 8.44 us -> 0 us
  matrix products: 7.39 us -> 0 us
  other arithmetic: 5.7 us -> 0 us
  local copies, waits for them, and re-layouts: 7.48 us -> 3.28 us
    psum x2 -> x0, blocking collectives: 80.3 us -> none  [local(): distance_sq = lax.psum(distance_sq, ('client', 'param'))]
    pallas_call x0 -> x1, Pallas kernels: none -> 59.3 us  [local(): pl.pallas_call(functools.partial(kernel, groups, members, cores, chunks),...]
    unnamed x1 -> x0, blocking collectives: 41.2 us -> none
    all_to_all x1 -> x0, starting transfers between devices: 8.44 us -> none  [local(): lax.all_to_all(updates, 'client', split_axis=1, concat_axis=0, tiled=True)]
    dot_general x3 -> x0, matrix products: 7.39 us -> none  [weighted_sum(): jnp.einsum('c,crk->rk', weights, updates, precision=lax.Precision.HIGHEST)]
    div x4 -> x0, other arithmetic: 3.24 us -> none  [the longest x3 2.59 us: local(): median = weighted_sum(weights, exchanged) / weight_sum]
    unnamed x10 -> x6, local copies, waits for them, and re-layouts: 6.25 us -> 3.28 us
    reduce_sum x5 -> x0, other arithmetic: 2.46 us -> none  [the longest x3 1.82 us: local(): weight_sum = jnp.sum(weights)]
  transfers between devices with their start and end apart: 1 -> 0, of which waited for: 0 -> 0; matrix products, arithmetic and copies ran while one was open for 1% -> 0% of each run, Pallas kernels for 0% -> 0%
where the time goes in v1:
time: 63.4 us; the launch traced here: 63.2 us
  Pallas kernels  59.3 us (94%)
  local copies, waits for them, and re-layouts  3.28 us (5%)
  between operations  0.65 us (1%)
    pallas_call x1, Pallas kernels, local(): pl.pallas_call(functools.partial(kernel, groups, members, cores, chunks),...  59.3 us
    unnamed x6, local copies, waits for them, and re-layouts  3.28 us

profile of v1, /device:TPU:0, one launch (start us, length us, event | category | flops | bytes accessed | tf_op | source)
XLA Modules:
  0.0 63.2 jit_solution(7767354249759885555)
XLA Ops:
  0.6 0.0 copy-start
  0.6 1.5 %copy-done = f32[2,128,1792]{2,1,0:T(8,128)S(1)} copy-done((f32[2,128,1792]{2,1,0:T(8,128)S(1)}, f32[2,128,1792]{2,1,0:T(8,128)}, u32[]{:S(2)}) %copy-start) | copy-done | bytes 1835032
  2.1 0.0 copy-start.1
  2.1 0.7 %copy-done.1 = s32[2]{0:T(128)S(1)} copy-done((s32[2]{0:T(128)S(1)}, s32[2]{0:T(128)}, u32[]{:S(2)}) %copy-start.1) | copy-done | bytes 32
  2.8 59.3 %shard_map.41 = (f32[8,1792]{1,0:T(8,128)S(1)}, f32[2]{0:T(128)S(1)}) custom-call(f32[2,2,8,8,1792]{4,3,2,1,0:T(8,128)S(1)} %bitcast.1, s32[2]{0:T(128)S(1)} %copy-done.1), custom_call_target="tpu_custom_call" | custom-call | flops 7340032 | bytes 3670016 | tf_op jit(solution)/shard_map/pallas_call | solution.py:257
  62.1 0.6 copy.6
  62.7 0.5 copy.7
Async XLA Ops:
  0.6 1.5 %copy-start = (f32[2,128,1792]{2,1,0:T(8,128)S(1)}, f32[2,128,1792]{2,1,0:T(8,128)}, u32[]{:S(2)}) copy-start(f32[2,128,1792]{2,1,0:T(8,128)} %param.2) | copy-start | bytes 5505028
  2.1 0.7 %copy-start.1 = (s32[2]{0:T(128)S(1)}, s32[2]{0:T(128)}, u32[]{:S(2)}) copy-start(s32[2]{0:T(128)} %cnt_ref.1) | copy-start | bytes 28

commit v2 on v1

--- a/solution.py
+++ b/solution.py
@@ -11,7 +11,7 @@
 LANES = 128
 SUBLANES = 8
 GROUPS = 2
-CHUNKS = 2
+CHUNK_ENDS = (0.43, 0.79, 1.0)
 
 smoothing = 1e-06
 
@@ -38,16 +38,19 @@
     return (median, shares)
 
 
-def kernel(groups, members, cores, chunks, u_ref, cnt_ref, med_ref, share_ref,
-           held, cnt_send, cnt_held, dist_send, dist_held, dist_rows, weight, part, part_in, last, last_in,
-           own_sem, u_send, u_recv, c_send, c_recv, p_send, p_recv, l_send, l_recv, d_send, d_recv):
+def kernel(groups, members, cores, bounds, u_ref, cnt_hbm, med_ref, share_ref,
+           held, cnt_ref, cnt_send, cnt_held, dist_send, dist_held, dist_rows, weight, part, part_in, last, last_in,
+           in_sem, own_sem, u_send, u_recv, c_send, c_recv, p_send, p_recv, l_send, l_recv, d_send, d_recv):
     nc, cols = u_ref.shape[0], u_ref.shape[-1]
     clients = nc * members
     me, core = lax.axis_index("client"), lax.axis_index("param")
     j, h = lax.rem(me, members), lax.div(me, members)
     partner = lax.rem(me + members, groups * members)
     rank = core * members + j
-    width = cols // chunks
+    chunks = len(bounds) - 1
+
+    def lanes(k, extra=0):
+        return pl.ds(bounds[k] * LANES, (bounds[k + 1] - bounds[k]) * LANES + extra)
 
     def member(o, c):
         return {"client": h * members + lax.rem(j + o, members), "param": lax.rem(core + c, cores)}
@@ -58,25 +61,41 @@
         pl.semaphore_signal(barrier, inc=1, device_id=member(o, c), device_id_type=pl.DeviceIdType.MESH)
     if groups > 1:
         pl.semaphore_signal(barrier, inc=1, device_id={"client": partner}, device_id_type=pl.DeviceIdType.MESH)
+    counts_in = pltpu.make_async_copy(cnt_hbm, cnt_ref, in_sem)
+    counts_in.start()
     own = []
     for k in range(chunks):
-        sl = pl.ds(k * width, width)
+        sl = lanes(k)
         own.append(pltpu.make_async_copy(u_ref.at[:, :, j, :, sl], held.at[j, :, :, :, sl], own_sem.at[k]))
         own[-1].start()
+    counts_in.wait()
     for c in range(nc):
         row = jnp.full((1, LANES), cnt_ref[c], jnp.int32).astype(jnp.float32)
         cnt_send[c:c + 1, :] = row
         cnt_held[j, c:c + 1, :] = row
     pl.semaphore_wait(barrier, len(others) + (groups > 1))
 
+    full = members - 1
+    masks = [m for low in range(1, members // 2) for m in (low, full - low)] + [full]
+    bits = [1 << b for b in range(full.bit_length())]
+
+    def peer(o):
+        m, index = masks[o - 1], 0
+        for b in bits:
+            flip = (m // b) % 2
+            if m != full:
+                flip = flip + lax.rem(core, 2) * (1 - 2 * flip)
+            index = index + b * lax.rem(lax.rem(lax.div(j, b), 2) + flip, 2)
+        return index
+
     def count_copy(o, slot):
         return pltpu.make_async_remote_copy(
             src_ref=cnt_send, dst_ref=cnt_held.at[slot], send_sem=c_send.at[o], recv_sem=c_recv.at[o],
-            device_id={"client": h * members + lax.rem(j + o, members)}, device_id_type=pl.DeviceIdType.MESH)
+            device_id={"client": h * members + peer(o)}, device_id_type=pl.DeviceIdType.MESH)
 
     def rows_copy(o, k, slot):
-        to = lax.rem(j + o, members)
-        sl = pl.ds(k * width, width)
+        to = peer(o)
+        sl = lanes(k)
         return pltpu.make_async_remote_copy(
             src_ref=u_ref.at[:, :, to, :, sl], dst_ref=held.at[slot, :, :, :, sl],
             send_sem=u_send.at[o, k], recv_sem=u_recv.at[o, k],
@@ -92,7 +111,7 @@
             rows_copy(o, k, j).start()
 
     def part_copy(i, k):
-        sl = pl.ds(k * width, width + (LANES if k == chunks - 1 else 0))
+        sl = lanes(k, LANES if k == chunks - 1 else 0)
         return pltpu.make_async_remote_copy(
             src_ref=part.at[i, :, :, sl], dst_ref=part_in.at[i, :, :, sl],
             send_sem=p_send.at[i, k], recv_sem=p_recv.at[i, k],
@@ -122,14 +141,14 @@
             if i == 0:
                 own[k].wait()
                 for o in range(1, members):
-                    rows_copy(o, k, source(o)).wait_recv()
+                    rows_copy(o, k, peer(o)).wait_recv()
 
             def body(t, carry):
                 for r in range(groups):
                     part[i, r, :, tile(t)] = sum_tile(w, r, t)
                 return carry
 
-            lax.fori_loop(k * width // LANES, (k + 1) * width // LANES, body, 0)
+            lax.fori_loop(bounds[k], bounds[k + 1], body, 0)
             if groups > 1:
                 part_copy(i, k).start()
 
@@ -156,7 +175,7 @@
                         acc[c] = acc[c] + d * d
                 return tuple(acc)
 
-            acc = lax.fori_loop(k * width // LANES, (k + 1) * width // LANES, body, acc)
+            acc = lax.fori_loop(bounds[k], bounds[k + 1], body, acc)
         for c in range(clients):
             dist_rows[c:c + 1, :] = jnp.sum(acc[c], axis=0, keepdims=True)
         eye = (lax.broadcasted_iota(jnp.int32, (clients, LANES), 0)
@@ -187,7 +206,7 @@
             copy(n, o, c, rank).wait_send()
 
     for o in range(1, members):
-        count_copy(o, source(o)).wait_recv()
+        count_copy(o, peer(o)).wait_recv()
     for c in range(clients):
         weight[c:c + 1, :] = cnt_held[c // nc, c % nc:c % nc + 1, :]
     for i in range(ITERS):
@@ -246,21 +265,24 @@
     devices, cores = lax.axis_size("client"), lax.axis_size("param")
     groups = GROUPS if devices % GROUPS == 0 and devices > GROUPS else 1
     members = devices // groups
-    chunks = CHUNKS if cols % (CHUNKS * LANES) == 0 else 1
+    tiles = cols // LANES
+    bounds = sorted({0, tiles} | {round(end * tiles) for end in CHUNK_ENDS})
+    chunks = len(bounds) - 1
     mine = rows // devices
-    if rows % devices or mine != SUBLANES or cols % LANES or members < 2 or nc * members > LANES:
+    if rows % devices or mine != SUBLANES or cols % LANES or members < 2 or members & (members - 1) or nc * members > LANES:
         return local_plain(updates, sample_counts)
     clients = nc * members
     f32 = jnp.float32
     dma = pltpu.SemaphoreType.DMA
     wide = cols + LANES
     return pl.pallas_call(
-        functools.partial(kernel, groups, members, cores, chunks),
+        functools.partial(kernel, groups, members, cores, bounds),
         out_shape=(jax.ShapeDtypeStruct((mine, cols), f32), jax.ShapeDtypeStruct((nc,), f32)),
-        in_specs=[pl.BlockSpec(memory_space=pl.ANY), pl.BlockSpec(memory_space=pltpu.SMEM)],
+        in_specs=[pl.BlockSpec(memory_space=pltpu.HBM)] * 2,
         out_specs=(pl.BlockSpec(memory_space=pltpu.VMEM), pl.BlockSpec(memory_space=pltpu.SMEM)),
         scratch_shapes=[
             pltpu.VMEM((members, nc, groups, mine, cols), f32),
+            pltpu.SMEM((nc,), jnp.int32),
             pltpu.VMEM((nc, LANES), f32),
             pltpu.VMEM((members, nc, LANES), f32),
             pltpu.VMEM((ITERS, 1, LANES), f32),
@@ -271,6 +293,7 @@
             pltpu.VMEM((ITERS, groups, mine, wide), f32),
             pltpu.VMEM((mine, wide), f32),
             pltpu.VMEM((mine, wide), f32),
+            dma,
             dma((chunks,)),
             dma((members, chunks)),
             dma((members, chunks)),
@@ -284,7 +307,7 @@
             dma((ITERS, cores * members)),
         ],
         compiler_params=pltpu.CompilerParams(
-            collective_id=0, has_side_effects=True, vmem_limit_bytes=32 * 1024 * 1024),
+            collective_id=0, has_side_effects=True, vmem_limit_bytes=56 * 1024 * 1024),
         cost_estimate=pl.CostEstimate(
             flops=16 * clients * groups * mine * cols, bytes_accessed=8 * nc * rows * cols, transcendentals=0),
     )(updates.reshape(nc, groups, members, mine, cols), sample_counts)

time: 63.4 us -> 59.8 us (0.943)
  Pallas kernels: 59.3 us -> 56.4 us
  local copies, waits for them, and re-layouts: 3.28 us -> 2.56 us
    pallas_call x1, Pallas kernels: 59.3 us -> 56.4 us  [local(): pl.pallas_call(functools.partial(kernel, groups, members, cores, bounds),...]
    unnamed x6 -> x2, local copies, waits for them, and re-layouts: 3.28 us -> 2.56 us
where the time goes in v2:
time: 59.8 us; the launch traced here: 59.6 us
  Pallas kernels  56.4 us (94%)
  local copies, waits for them, and re-layouts  2.56 us (4%)
  between operations  0.64 us (1%)
    pallas_call x1, Pallas kernels, local(): pl.pallas_call(functools.partial(kernel, groups, members, cores, bounds),...  56.4 us
    unnamed x2, local copies, waits for them, and re-layouts  2.56 us

profile of v2, /device:TPU:0, one launch (start us, length us, event | category | flops | bytes accessed | tf_op | source)
XLA Modules:
  0.0 59.6 jit_solution(547260650591416590)
XLA Ops:
  0.6 56.4 %shard_map.41 = (f32[8,1792]{1,0:T(8,128)}, f32[2]{0:T(128)}) custom-call(f32[2,2,8,8,1792]{4,3,2,1,0:T(8,128)} %bitcast.1, s32[2]{0:T(128)} %cnt_hbm.1), custom_call_target="tpu_custom_call" | custom-call | flops 7340032 | bytes 3670016 | tf_op jit(solution)/shard_map/pallas_call | solution.py:278
  57.0 1.4 %copy.6 = f32[8,1792]{1,0:T(8,128)} copy(f32[8,1792]{1,0:T(8,128)} %get-tuple-element.4) | data formatting | bytes 114688
  58.5 1.1 %copy.7 = f32[2]{0:T(128)} copy(f32[2]{0:T(128)} %get-tuple-element.5) | data formatting | bytes 16

commit v3 on v2

--- a/solution.py
+++ b/solution.py
@@ -49,8 +49,8 @@
     rank = core * members + j
     chunks = len(bounds) - 1
 
-    def lanes(k, extra=0):
-        return pl.ds(bounds[k] * LANES, (bounds[k + 1] - bounds[k]) * LANES + extra)
+    def lanes(k):
+        return pl.ds(bounds[k] * LANES, (bounds[k + 1] - bounds[k]) * LANES)
 
     def member(o, c):
         return {"client": h * members + lax.rem(j + o, members), "param": lax.rem(core + c, cores)}
@@ -68,11 +68,6 @@
         sl = lanes(k)
         own.append(pltpu.make_async_copy(u_ref.at[:, :, j, :, sl], held.at[j, :, :, :, sl], own_sem.at[k]))
         own[-1].start()
-    counts_in.wait()
-    for c in range(nc):
-        row = jnp.full((1, LANES), cnt_ref[c], jnp.int32).astype(jnp.float32)
-        cnt_send[c:c + 1, :] = row
-        cnt_held[j, c:c + 1, :] = row
     pl.semaphore_wait(barrier, len(others) + (groups > 1))
 
     full = members - 1
@@ -104,18 +99,31 @@
     def source(o):
         return lax.rem(j + members - o, members)
 
-    for o in range(1, members):
-        count_copy(o, j).start()
     for k in range(chunks):
         for o in range(1, members):
             rows_copy(o, k, j).start()
+        if k == 0:
+            counts_in.wait()
+            for c in range(nc):
+                row = jnp.full((1, LANES), cnt_ref[c], jnp.int32).astype(jnp.float32)
+                cnt_send[c:c + 1, :] = row
+                cnt_held[j, c:c + 1, :] = row
+            for o in range(1, members):
+                count_copy(o, j).start()
 
     def part_copy(i, k):
-        sl = lanes(k, LANES if k == chunks - 1 else 0)
+        first = bounds[k] + (k > 0)
+        sl = pl.ds(first * LANES, (bounds[k + 1] + 1 - first) * LANES)
         return pltpu.make_async_remote_copy(
             src_ref=part.at[i, :, :, sl], dst_ref=part_in.at[i, :, :, sl],
             send_sem=p_send.at[i, k], recv_sem=p_recv.at[i, k],
             device_id={"client": partner}, device_id_type=pl.DeviceIdType.MESH)
+
+    def dist_copy(i, n, o, c, slot):
+        return pltpu.make_async_remote_copy(
+            src_ref=dist_send.at[i], dst_ref=dist_held.at[i, slot],
+            send_sem=d_send.at[i, n], recv_sem=d_recv.at[i, n],
+            device_id=member(o, c), device_id_type=pl.DeviceIdType.MESH)
 
     def weights_now():
         w = [jnp.broadcast_to(weight[c:c + 1, :], (SUBLANES, LANES)) for c in range(clients)]
@@ -127,55 +135,78 @@
     def tile(t):
         return pl.ds(pl.multiple_of(t * LANES, LANES), LANES)
 
+    def after(t):
+        return pl.ds(pl.multiple_of((t + 1) * LANES, LANES), LANES)
+
     def sum_tile(w, r, t):
-        acc = w[0] * held[0, 0, r, :, tile(t)]
-        for c in range(1, clients):
-            acc = acc + w[c] * held[c // nc, c % nc, r, :, tile(t)]
-        return acc
-
-    def send_part(i):
+        sums = []
+        for c in range(clients):
+            x = w[c] * held[c // nc, c % nc, r, :, tile(t)]
+            if c < 4:
+                sums.append(x)
+            else:
+                sums[c % 4] = sums[c % 4] + x
+        while len(sums) > 1:
+            sums = [sums[n] + sums[n + 1] if n + 1 < len(sums) else sums[n] for n in range(0, len(sums), 2)]
+        return sums[0]
+
+    def iteration(i):
         w, total = weights_now()
         for r in range(groups):
-            part[i, r, :, pl.ds(cols, LANES)] = total
+            part[i, r, :, pl.ds(0, LANES)] = total
+
+        def send_part(k):
+            def body(t, carry):
+                for r in range(groups):
+                    part[i, r, :, after(t)] = sum_tile(w, r, t)
+                return carry
+
+            lax.fori_loop(bounds[k], bounds[k + 1], body, 0)
+            if groups > 1:
+                part_copy(i, k).start()
+
+        def add_distances(k, inverse, acc):
+            if groups > 1:
+                part_copy(i, k).wait_recv()
+            if inverse is None:
+                whole = part[i, 0, :, pl.ds(0, LANES)]
+                if groups > 1:
+                    whole = whole + part_in[i, 0, :, pl.ds(0, LANES)]
+                inverse = 1.0 / whole
+
+            def body(t, acc):
+                acc = list(acc)
+                for r in range(groups):
+                    m = part[i, r, :, after(t)]
+                    if groups > 1:
+                        m = m + part_in[i, r, :, after(t)]
+                    m = m * inverse
+                    for c in range(clients):
+                        d = held[c // nc, c % nc, r, :, tile(t)] - m
+                        acc[c] = acc[c] + d * d
+                return tuple(acc)
+
+            return inverse, lax.fori_loop(bounds[k], bounds[k + 1], body, acc)
+
+        inverse, acc = None, tuple(jnp.zeros((SUBLANES, LANES), jnp.float32) for _ in range(clients))
         for k in range(chunks):
             if i == 0:
                 own[k].wait()
                 for o in range(1, members):
                     rows_copy(o, k, peer(o)).wait_recv()
-
-            def body(t, carry):
-                for r in range(groups):
-                    part[i, r, :, tile(t)] = sum_tile(w, r, t)
-                return carry
-
-            lax.fori_loop(bounds[k], bounds[k + 1], body, 0)
-            if groups > 1:
-                part_copy(i, k).start()
-
-    def distances(i):
-        total = part[i, 0, :, pl.ds(cols, LANES)]
-        acc = tuple(jnp.zeros((SUBLANES, LANES), jnp.float32) for _ in range(clients))
-        if groups > 1:
-            part_copy(i, chunks - 1).wait_recv()
-            total = total + part_in[i, 0, :, pl.ds(cols, LANES)]
-        inverse = 1.0 / total
-        for k in range(chunks):
-            if groups > 1 and k < chunks - 1:
-                part_copy(i, k).wait_recv()
-
-            def body(t, acc):
-                acc = list(acc)
-                for r in range(groups):
-                    m = part[i, r, :, tile(t)]
-                    if groups > 1:
-                        m = m + part_in[i, r, :, tile(t)]
-                    m = m * inverse
-                    for c in range(clients):
-                        d = held[c // nc, c % nc, r, :, tile(t)] - m
-                        acc[c] = acc[c] + d * d
-                return tuple(acc)
-
-            acc = lax.fori_loop(bounds[k], bounds[k + 1], body, acc)
+            send_part(k)
+            if i == 0 and k > 0:
+                inverse, acc = add_distances(k - 1, inverse, acc)
+        if i == 1:
+            for o in range(1, members):
+                count_copy(o, j).wait_send()
+                for k in range(chunks):
+                    rows_copy(o, k, j).wait_send()
+        if i > 0:
+            for n, (o, c) in enumerate(others):
+                dist_copy(i - 1, n, o, c, rank).wait_send()
+        for k in range(chunks - 1 if i == 0 else 0, chunks):
+            inverse, acc = add_distances(k, inverse, acc)
         for c in range(clients):
             dist_rows[c:c + 1, :] = jnp.sum(acc[c], axis=0, keepdims=True)
         eye = (lax.broadcasted_iota(jnp.int32, (clients, LANES), 0)
@@ -185,16 +216,10 @@
         dist_send[i] = row
         dist_held[i, rank] = row
 
-        def copy(n, o, c, slot):
-            return pltpu.make_async_remote_copy(
-                src_ref=dist_send.at[i], dst_ref=dist_held.at[i, slot],
-                send_sem=d_send.at[i, n], recv_sem=d_recv.at[i, n],
-                device_id=member(o, c), device_id_type=pl.DeviceIdType.MESH)
-
         for n, (o, c) in enumerate(others):
-            copy(n, o, c, rank).start()
+            dist_copy(i, n, o, c, rank).start()
         for n, (o, c) in enumerate(others):
-            copy(n, o, c, lax.rem(core + cores - c, cores) * members + source(o)).wait_recv()
+            dist_copy(i, n, o, c, lax.rem(core + cores - c, cores) * members + source(o)).wait_recv()
         row = dist_held[i, 0]
         for s in range(1, cores * members):
             row = row + dist_held[i, s]
@@ -202,26 +227,23 @@
         root = jnp.sqrt(jnp.broadcast_to(column, eye.shape) + smoothing)
         for c in range(clients):
             weight[c:c + 1, :] = cnt_held[c // nc, c % nc:c % nc + 1, :] / root[c:c + 1, :]
-        for n, (o, c) in enumerate(others):
-            copy(n, o, c, rank).wait_send()
 
     for o in range(1, members):
         count_copy(o, peer(o)).wait_recv()
     for c in range(clients):
         weight[c:c + 1, :] = cnt_held[c // nc, c % nc:c % nc + 1, :]
     for i in range(ITERS):
-        send_part(i)
-        distances(i)
+        iteration(i)
 
     w, total = weights_now()
     final = pltpu.make_async_remote_copy(
         src_ref=last, dst_ref=last_in, send_sem=l_send, recv_sem=l_recv,
         device_id={"client": partner}, device_id_type=pl.DeviceIdType.MESH)
     if groups > 1:
-        last[:, pl.ds(cols, LANES)] = total
+        last[:, pl.ds(0, LANES)] = total
 
         def body(t, carry):
-            last[:, tile(t)] = sum_tile(w, 1 - h, t)
+            last[:, after(t)] = sum_tile(w, 1 - h, t)
             return carry
 
         lax.fori_loop(0, cols // LANES, body, 0)
@@ -232,15 +254,20 @@
         return carry
 
     lax.fori_loop(0, cols // LANES, body, 0)
+    for n, (o, c) in enumerate(others):
+        dist_copy(ITERS - 1, n, o, c, rank).wait_send()
     if groups > 1:
+        for i in range(ITERS):
+            for k in range(chunks):
+                part_copy(i, k).wait_send()
         final.wait_recv()
-        total = total + last_in[:, pl.ds(cols, LANES)]
+        total = total + last_in[:, pl.ds(0, LANES)]
     inverse = 1.0 / total
 
     def body(t, carry):
         m = med_ref[:, tile(t)]
         if groups > 1:
-            m = m + last_in[:, tile(t)]
+            m = m + last_in[:, after(t)]
         med_ref[:, tile(t)] = m * inverse
         return carry
 
@@ -248,15 +275,7 @@
     for c in range(nc):
         share = (groups * clients) * weight[pl.ds(nc * j + c, 1), :] * inverse[0:1, :]
         share_ref[c] = share[0, 0]
-
-    for o in range(1, members):
-        count_copy(o, j).wait_send()
-        for k in range(chunks):
-            rows_copy(o, k, j).wait_send()
     if groups > 1:
-        for i in range(ITERS):
-            for k in range(chunks):
-                part_copy(i, k).wait_send()
         final.wait_send()
 
 
@@ -277,7 +296,7 @@
     wide = cols + LANES
     return pl.pallas_call(
         functools.partial(kernel, groups, members, cores, bounds),
-        out_shape=(jax.ShapeDtypeStruct((mine, cols), f32), jax.ShapeDtypeStruct((nc,), f32)),
+        out_shape=(pltpu.VMEM((mine, cols), f32), pltpu.SMEM((nc,), f32)),
         in_specs=[pl.BlockSpec(memory_space=pltpu.HBM)] * 2,
         out_specs=(pl.BlockSpec(memory_space=pltpu.VMEM), pl.BlockSpec(memory_space=pltpu.SMEM)),
         scratch_shapes=[

time: 59.8 us -> 56.8 us (0.950)
  Pallas kernels: 56.4 us -> 54.9 us
  local copies, waits for them, and re-layouts: 2.56 us -> 1.14 us
    pallas_call x1, Pallas kernels: 56.4 us -> 54.9 us  [local(): pl.pallas_call(functools.partial(kernel, groups, members, cores, bounds),...]
    unnamed x2, local copies, waits for them, and re-layouts: 2.56 us -> 1.14 us
where the time goes in v3:
time: 56.8 us; the launch traced here: 56.7 us
  Pallas kernels  54.9 us (97%)
  local copies, waits for them, and re-layouts  1.14 us (2%)
  between operations  0.64 us (1%)
    pallas_call x1, Pallas kernels, local(): pl.pallas_call(functools.partial(kernel, groups, members, cores, bounds),...  54.9 us
    unnamed x2, local copies, waits for them, and re-layouts  1.14 us

profile of v3, /device:TPU:0, one launch (start us, length us, event | category | flops | bytes accessed | tf_op | source)
XLA Modules:
  0.0 56.7 jit_solution(14728386978129552370)
XLA Ops:
  0.6 54.9 %shard_map.41 = (f32[8,1792]{1,0:T(8,128)S(1)}, f32[2]{0:T(128)S(4)}) custom-call(f32[2,2,8,8,1792]{4,3,2,1,0:T(8,128)} %bitcast.1, s32[2]{0:T(128)} %cnt_hbm.1), custom_call_target="tpu_custom_call" | custom-call | flops 7340032 | bytes 3670016 | tf_op jit(solution)/shard_map/pallas_call | solution.py:297
  55.5 0.6 %copy.6 = f32[8,1792]{1,0:T(8,128)} copy(f32[8,1792]{1,0:T(8,128)S(1)} %get-tuple-element.2) | data formatting | bytes 114688
  56.2 0.5 copy.7

commit v4 on v3

--- a/solution.py
+++ b/solution.py
@@ -11,7 +11,8 @@
 LANES = 128
 SUBLANES = 8
 GROUPS = 2
-CHUNK_ENDS = (0.43, 0.79, 1.0)
+CHUNK_ENDS = (0.5, 0.79, 0.93, 1.0)
+LAST_ENDS = (0.43, 1.0)
 
 smoothing = 1e-06
 
@@ -38,7 +39,7 @@
     return (median, shares)
 
 
-def kernel(groups, members, cores, bounds, u_ref, cnt_hbm, med_ref, share_ref,
+def kernel(groups, members, cores, bounds, ends, u_ref, cnt_hbm, med_ref, share_ref,
            held, cnt_ref, cnt_send, cnt_held, dist_send, dist_held, dist_rows, weight, part, part_in, last, last_in,
            in_sem, own_sem, u_send, u_recv, c_send, c_recv, p_send, p_recv, l_send, l_recv, d_send, d_recv):
     nc, cols = u_ref.shape[0], u_ref.shape[-1]
@@ -53,9 +54,15 @@
         return pl.ds(bounds[k] * LANES, (bounds[k + 1] - bounds[k]) * LANES)
 
     def member(o, c):
-        return {"client": h * members + lax.rem(j + o, members), "param": lax.rem(core + c, cores)}
-
-    others = [(o, c) for c in range(cores) for o in range(members) if o or c]
+        return {"client": h * members + flipped(o), "param": lax.rem(core + c, cores)}
+
+    def flipped(m):
+        return sum(b * lax.rem(lax.rem(lax.div(j, b), 2) + (m // b) % 2, 2) for b in bits)
+
+    full = members - 1
+    bits = [1 << b for b in range(full.bit_length())]
+    others = sorted(((o, c) for c in range(cores) for o in range(members) if o or c),
+                    key=lambda x: -bin(x[0]).count("1"))
     barrier = pltpu.get_barrier_semaphore()
     for o, c in others:
         pl.semaphore_signal(barrier, inc=1, device_id=member(o, c), device_id_type=pl.DeviceIdType.MESH)
@@ -70,9 +77,7 @@
         own[-1].start()
     pl.semaphore_wait(barrier, len(others) + (groups > 1))
 
-    full = members - 1
-    masks = [m for low in range(1, members // 2) for m in (low, full - low)] + [full]
-    bits = [1 << b for b in range(full.bit_length())]
+    masks = [full] + [m for low in range(members // 2 - 1, 0, -1) for m in (full - low, low)]
 
     def peer(o):
         m, index = masks[o - 1], 0
@@ -95,9 +100,6 @@
             src_ref=u_ref.at[:, :, to, :, sl], dst_ref=held.at[slot, :, :, :, sl],
             send_sem=u_send.at[o, k], recv_sem=u_recv.at[o, k],
             device_id={"client": h * members + to}, device_id_type=pl.DeviceIdType.MESH)
-
-    def source(o):
-        return lax.rem(j + members - o, members)
 
     for k in range(chunks):
         for o in range(1, members):
@@ -219,7 +221,7 @@
         for n, (o, c) in enumerate(others):
             dist_copy(i, n, o, c, rank).start()
         for n, (o, c) in enumerate(others):
-            dist_copy(i, n, o, c, lax.rem(core + cores - c, cores) * members + source(o)).wait_recv()
+            dist_copy(i, n, o, c, lax.rem(core + cores - c, cores) * members + flipped(o)).wait_recv()
         row = dist_held[i, 0]
         for s in range(1, cores * members):
             row = row + dist_held[i, s]
@@ -236,9 +238,13 @@
         iteration(i)
 
     w, total = weights_now()
-    final = pltpu.make_async_remote_copy(
-        src_ref=last, dst_ref=last_in, send_sem=l_send, recv_sem=l_recv,
-        device_id={"client": partner}, device_id_type=pl.DeviceIdType.MESH)
+    def final_copy(k):
+        first = ends[k] + (k > 0)
+        sl = pl.ds(first * LANES, (ends[k + 1] + 1 - first) * LANES)
+        return pltpu.make_async_remote_copy(
+            src_ref=last.at[:, sl], dst_ref=last_in.at[:, sl], send_sem=l_send.at[k], recv_sem=l_recv.at[k],
+            device_id={"client": partner}, device_id_type=pl.DeviceIdType.MESH)
+
     if groups > 1:
         last[:, pl.ds(0, LANES)] = total
 
@@ -246,8 +252,9 @@
             last[:, after(t)] = sum_tile(w, 1 - h, t)
             return carry
 
-        lax.fori_loop(0, cols // LANES, body, 0)
-        final.start()
+        for k in range(len(ends) - 1):
+            lax.fori_loop(ends[k], ends[k + 1], body, 0)
+            final_copy(k).start()
 
     def body(t, carry):
         med_ref[:, tile(t)] = sum_tile(w, h, t)
@@ -260,7 +267,7 @@
         for i in range(ITERS):
             for k in range(chunks):
                 part_copy(i, k).wait_send()
-        final.wait_recv()
+        final_copy(0).wait_recv()
         total = total + last_in[:, pl.ds(0, LANES)]
     inverse = 1.0 / total
 
@@ -271,12 +278,16 @@
         med_ref[:, tile(t)] = m * inverse
         return carry
 
-    lax.fori_loop(0, cols // LANES, body, 0)
+    for k in range(len(ends) - 1):
+        if groups > 1 and k > 0:
+            final_copy(k).wait_recv()
+        lax.fori_loop(ends[k], ends[k + 1], body, 0)
     for c in range(nc):
         share = (groups * clients) * weight[pl.ds(nc * j + c, 1), :] * inverse[0:1, :]
         share_ref[c] = share[0, 0]
     if groups > 1:
-        final.wait_send()
+        for k in range(len(ends) - 1):
+            final_copy(k).wait_send()
 
 
 def local(updates, sample_counts):
@@ -286,6 +297,7 @@
     members = devices // groups
     tiles = cols // LANES
     bounds = sorted({0, tiles} | {round(end * tiles) for end in CHUNK_ENDS})
+    ends = sorted({0, tiles} | {round(end * tiles) for end in LAST_ENDS})
     chunks = len(bounds) - 1
     mine = rows // devices
     if rows % devices or mine != SUBLANES or cols % LANES or members < 2 or members & (members - 1) or nc * members > LANES:
@@ -295,7 +307,7 @@
     dma = pltpu.SemaphoreType.DMA
     wide = cols + LANES
     return pl.pallas_call(
-        functools.partial(kernel, groups, members, cores, bounds),
+        functools.partial(kernel, groups, members, cores, bounds, ends),
         out_shape=(pltpu.VMEM((mine, cols), f32), pltpu.SMEM((nc,), f32)),
         in_specs=[pl.BlockSpec(memory_space=pltpu.HBM)] * 2,
         out_specs=(pl.BlockSpec(memory_space=pltpu.VMEM), pl.BlockSpec(memory_space=pltpu.SMEM)),
@@ -320,8 +332,8 @@
             dma((members,)),
             dma((ITERS, chunks)),
             dma((ITERS, chunks)),
-            dma,
-            dma,
+            dma((len(ends) - 1,)),
+            dma((len(ends) - 1,)),
             dma((ITERS, cores * members)),
             dma((ITERS, cores * members)),
         ],

time: 56.8 us -> 56.5 us (level)
  no operation moved by 1% of the time
where the time goes in v4:
time: 56.5 us; the launch traced here: 56.4 us
  Pallas kernels  54.6 us (97%)
  local copies, waits for them, and re-layouts  1.14 us (2%)
  between operations  0.64 us (1%)
    pallas_call x1, Pallas kernels, local(): pl.pallas_call(functools.partial(kernel, groups, members, cores, bounds,...  54.6 us
    unnamed x2, local copies, waits for them, and re-layouts  1.14 us

profile of v4, /device:TPU:0, one launch (start us, length us, event | category | flops | bytes accessed | tf_op | source)
XLA Modules:
  0.0 56.4 jit_solution(9003013129859450687)
XLA Ops:
  0.6 54.6 %shard_map.41 = (f32[8,1792]{1,0:T(8,128)S(1)}, f32[2]{0:T(128)S(4)}) custom-call(f32[2,2,8,8,1792]{4,3,2,1,0:T(8,128)} %bitcast.1, s32[2]{0:T(128)} %cnt_hbm.1), custom_call_target="tpu_custom_call" | custom-call | flops 7340032 | bytes 3670016 | tf_op jit(solution)/shard_map/pallas_call | solution.py:309
  55.2 0.6 %copy.6 = f32[8,1792]{1,0:T(8,128)} copy(f32[8,1792]{1,0:T(8,128)S(1)} %get-tuple-element.2) | data formatting | bytes 114688
  55.9 0.5 copy.7

commit v5 on v4

--- a/solution.py
+++ b/solution.py
@@ -11,7 +11,8 @@
 LANES = 128
 SUBLANES = 8
 GROUPS = 2
-CHUNK_ENDS = (0.5, 0.79, 0.93, 1.0)
+CHUNK_TILES = 2
+IN_FLIGHT = 3
 LAST_ENDS = (0.43, 1.0)
 
 smoothing = 1e-06
@@ -101,7 +102,7 @@
             send_sem=u_send.at[o, k], recv_sem=u_recv.at[o, k],
             device_id={"client": h * members + to}, device_id_type=pl.DeviceIdType.MESH)
 
-    for k in range(chunks):
+    for k in range(min(IN_FLIGHT, chunks)):
         for o in range(1, members):
             rows_copy(o, k, j).start()
         if k == 0:
@@ -196,6 +197,8 @@
                 own[k].wait()
                 for o in range(1, members):
                     rows_copy(o, k, peer(o)).wait_recv()
+                    if k + IN_FLIGHT < chunks:
+                        rows_copy(o, k + IN_FLIGHT, j).start()
             send_part(k)
             if i == 0 and k > 0:
                 inverse, acc = add_distances(k - 1, inverse, acc)
@@ -296,7 +299,7 @@
     groups = GROUPS if devices % GROUPS == 0 and devices > GROUPS else 1
     members = devices // groups
     tiles = cols // LANES
-    bounds = sorted({0, tiles} | {round(end * tiles) for end in CHUNK_ENDS})
+    bounds = sorted({tiles, *range(0, tiles, CHUNK_TILES)})
     ends = sorted({0, tiles} | {round(end * tiles) for end in LAST_ENDS})
     chunks = len(bounds) - 1
     mine = rows // devices

time: 56.5 us -> 56.9 us (level)
  no operation moved by 1% of the time
where the time goes in v5:
time: 56.9 us; the launch traced here: 56.8 us
  Pallas kernels  55 us (97%)
  local copies, waits for them, and re-layouts  1.14 us (2%)
  between operations  0.64 us (1%)
    pallas_call x1, Pallas kernels, local(): pl.pallas_call(functools.partial(kernel, groups, members, cores, bounds,...  55 us
    unnamed x2, local copies, waits for them, and re-layouts  1.14 us

profile of v5, /device:TPU:0, one launch (start us, length us, event | category | flops | bytes accessed | tf_op | source)
XLA Modules:
  0.0 56.8 jit_solution(17240457481656240635)
XLA Ops:
  0.6 55.0 %shard_map.41 = (f32[8,1792]{1,0:T(8,128)S(1)}, f32[2]{0:T(128)S(4)}) custom-call(f32[2,2,8,8,1792]{4,3,2,1,0:T(8,128)} %bitcast.1, s32[2]{0:T(128)} %cnt_hbm.1), custom_call_target="tpu_custom_call" | custom-call | flops 7340032 | bytes 3670016 | tf_op jit(solution)/shard_map/pallas_call | solution.py:312
  55.6 0.6 %copy.6 = f32[8,1792]{1,0:T(8,128)} copy(f32[8,1792]{1,0:T(8,128)S(1)} %get-tuple-element.2) | data formatting | bytes 114688
  56.2 0.5 copy.7

commit v6 on v5

--- a/solution.py
+++ b/solution.py
@@ -41,8 +41,9 @@
 
 
 def kernel(groups, members, cores, bounds, ends, u_ref, cnt_hbm, med_ref, share_ref,
-           held, cnt_ref, cnt_send, cnt_held, dist_send, dist_held, dist_rows, weight, part, part_in, last, last_in,
-           in_sem, own_sem, u_send, u_recv, c_send, c_recv, p_send, p_recv, l_send, l_recv, d_send, d_recv):
+           held, cnt_ref, cnt_send, cnt_held, dist_send, dist_held, dist_rows, weight, part, part_in, last, last_in, pre_u, pre, pre_in,
+           in_sem, own_sem, u_send, u_recv, c_send, c_recv, p_send, p_recv, l_send, l_recv, d_send, d_recv,
+           pre_sem, pre_send, pre_recv):
     nc, cols = u_ref.shape[0], u_ref.shape[-1]
     clients = nc * members
     me, core = lax.axis_index("client"), lax.axis_index("param")
@@ -68,7 +69,9 @@
     for o, c in others:
         pl.semaphore_signal(barrier, inc=1, device_id=member(o, c), device_id_type=pl.DeviceIdType.MESH)
     if groups > 1:
-        pl.semaphore_signal(barrier, inc=1, device_id={"client": partner}, device_id_type=pl.DeviceIdType.MESH)
+        for m in range(members):
+            pl.semaphore_signal(barrier, inc=1, device_id={"client": (1 - h) * members + flipped(m)},
+                                device_id_type=pl.DeviceIdType.MESH)
     counts_in = pltpu.make_async_copy(cnt_hbm, cnt_ref, in_sem)
     counts_in.start()
     own = []
@@ -76,7 +79,10 @@
         sl = lanes(k)
         own.append(pltpu.make_async_copy(u_ref.at[:, :, j, :, sl], held.at[j, :, :, :, sl], own_sem.at[k]))
         own[-1].start()
-    pl.semaphore_wait(barrier, len(others) + (groups > 1))
+    early = pltpu.make_async_copy(u_ref.at[:, :, :, :, lanes(chunks - 1)], pre_u, pre_sem)
+    if groups > 1:
+        early.start()
+    pl.semaphore_wait(barrier, len(others) + (members if groups > 1 else 0))
 
     masks = [full] + [m for low in range(members // 2 - 1, 0, -1) for m in (full - low, low)]
 
@@ -114,6 +120,26 @@
             for o in range(1, members):
                 count_copy(o, j).start()
 
+    def pre_copy(m, slot):
+        return pltpu.make_async_remote_copy(
+            src_ref=pre.at[flipped(m)], dst_ref=pre_in.at[slot], send_sem=pre_send.at[m], recv_sem=pre_recv.at[m],
+            device_id={"client": (1 - h) * members + flipped(m)}, device_id_type=pl.DeviceIdType.MESH)
+
+    if groups > 1:
+        early.wait()
+
+        def presum(q, carry):
+            for r in range(groups):
+                x = cnt_send[0:1, 0:1] * pre_u[0, r, q]
+                for c in range(1, nc):
+                    x = x + cnt_send[c:c + 1, 0:1] * pre_u[c, r, q]
+                pre[q, r] = x
+            return carry
+
+        lax.fori_loop(0, members, presum, 0)
+        for m in reversed(range(members)):
+            pre_copy(m, j).start()
+
     def part_copy(i, k):
         first = bounds[k] + (k > 0)
         sl = pl.ds(first * LANES, (bounds[k + 1] + 1 - first) * LANES)
@@ -153,6 +179,9 @@
             sums = [sums[n] + sums[n + 1] if n + 1 < len(sums) else sums[n] for n in range(0, len(sums), 2)]
         return sums[0]
 
+    def exchanged(i, k):
+        return groups > 1 and not (i == 0 and 0 < k == chunks - 1)
+
     def iteration(i):
         w, total = weights_now()
         for r in range(groups):
@@ -165,11 +194,19 @@
                 return carry
 
             lax.fori_loop(bounds[k], bounds[k + 1], body, 0)
-            if groups > 1:
+            if exchanged(i, k):
                 part_copy(i, k).start()
+            elif groups > 1:
+                for m in range(members):
+                    pre_copy(m, flipped(m)).wait_recv()
+                for r in range(groups):
+                    x = pre_in[0, r]
+                    for q in range(1, members):
+                        x = x + pre_in[q, r]
+                    part_in[i, r, :, pl.ds((bounds[k] + 1) * LANES, (bounds[k + 1] - bounds[k]) * LANES)] = x
 
         def add_distances(k, inverse, acc):
-            if groups > 1:
+            if exchanged(i, k):
                 part_copy(i, k).wait_recv()
             if inverse is None:
                 whole = part[i, 0, :, pl.ds(0, LANES)]
@@ -203,6 +240,9 @@
             if i == 0 and k > 0:
                 inverse, acc = add_distances(k - 1, inverse, acc)
         if i == 1:
+            if groups > 1:
+                for m in range(members):
+                    pre_copy(m, j).wait_send()
             for o in range(1, members):
                 count_copy(o, j).wait_send()
                 for k in range(chunks):
@@ -269,7 +309,8 @@
     if groups > 1:
         for i in range(ITERS):
             for k in range(chunks):
-                part_copy(i, k).wait_send()
+                if exchanged(i, k):
+                    part_copy(i, k).wait_send()
         final_copy(0).wait_recv()
         total = total + last_in[:, pl.ds(0, LANES)]
     inverse = 1.0 / total
@@ -303,12 +344,13 @@
     ends = sorted({0, tiles} | {round(end * tiles) for end in LAST_ENDS})
     chunks = len(bounds) - 1
     mine = rows // devices
-    if rows % devices or mine != SUBLANES or cols % LANES or members < 2 or members & (members - 1) or nc * members > LANES:
+    if rows % devices or mine != SUBLANES or cols % LANES or members < 2 or members & (members - 1) or tiles <= CHUNK_TILES or nc * members > LANES:
         return local_plain(updates, sample_counts)
     clients = nc * members
     f32 = jnp.float32
     dma = pltpu.SemaphoreType.DMA
     wide = cols + LANES
+    tail = (tiles - bounds[-2]) * LANES
     return pl.pallas_call(
         functools.partial(kernel, groups, members, cores, bounds, ends),
         out_shape=(pltpu.VMEM((mine, cols), f32), pltpu.SMEM((nc,), f32)),
@@ -327,6 +369,9 @@
             pltpu.VMEM((ITERS, groups, mine, wide), f32),
             pltpu.VMEM((mine, wide), f32),
             pltpu.VMEM((mine, wide), f32),
+            pltpu.VMEM((nc, groups, members, mine, tail), f32),
+            pltpu.VMEM((members, groups, mine, tail), f32),
+            pltpu.VMEM((members, groups, mine, tail), f32),
             dma,
             dma((chunks,)),
             dma((members, chunks)),
@@ -339,6 +384,9 @@
             dma((len(ends) - 1,)),
             dma((ITERS, cores * members)),
             dma((ITERS, cores * members)),
+            dma,
+            dma((members,)),
+            dma((members,)),
         ],
         compiler_params=pltpu.CompilerParams(
             collective_id=0, has_side_effects=True, vmem_limit_bytes=56 * 1024 * 1024),

time: 56.9 us -> 61 us (1.072)
  Pallas kernels: 55 us -> 59.1 us
    pallas_call x1, Pallas kernels: 55 us -> 59.1 us  [local(): pl.pallas_call(functools.partial(kernel, groups, members, cores, bounds,...]
where the time goes in v6:
time: 61 us; the launch traced here: 60.9 us
  Pallas kernels  59.1 us (97%)
  local copies, waits for them, and re-layouts  1.14 us (2%)
  between operations  0.64 us (1%)
    pallas_call x1, Pallas kernels, local(): pl.pallas_call(functools.partial(kernel, groups, members, cores, bounds,...  59.1 us

profile of v6, /device:TPU:0, one launch (start us, length us, event | category | flops | bytes accessed | tf_op | source)
XLA Modules:
  0.0 60.9 jit_solution(11773233568951779093)
XLA Ops:
  0.6 59.1 %shard_map.41 = (f32[8,1792]{1,0:T(8,128)S(1)}, f32[2]{0:T(128)S(4)}) custom-call(f32[2,2,8,8,1792]{4,3,2,1,0:T(8,128)} %bitcast.1, s32[2]{0:T(128)} %cnt_hbm.1), custom_call_target="tpu_custom_call" | custom-call | flops 7340032 | bytes 3670016 | tf_op jit(solution)/shard_map/pallas_call | solution.py:354
  59.7 0.6 %copy.6 = f32[8,1792]{1,0:T(8,128)} copy(f32[8,1792]{1,0:T(8,128)S(1)} %get-tuple-element.2) | data formatting | bytes 114688
  60.4 0.5 copy.7

commit v7 on v4

--- a/solution.py
+++ b/solution.py
@@ -11,7 +11,7 @@
 LANES = 128
 SUBLANES = 8
 GROUPS = 2
-CHUNK_ENDS = (0.5, 0.79, 0.93, 1.0)
+CHUNK_ENDS = (0.57, 1.0)
 LAST_ENDS = (0.43, 1.0)
 
 smoothing = 1e-06
@@ -53,19 +53,30 @@
     def lanes(k):
         return pl.ds(bounds[k] * LANES, (bounds[k + 1] - bounds[k]) * LANES)
 
-    def member(o, c):
+    bits = [1 << b for b in range((members - 1).bit_length())]
+
+    def flipped(m):
+        return sum(b * lax.rem(lax.rem(lax.div(j, b), 2) + lax.rem(lax.div(m, b), 2), 2) for b in bits)
+
+    def member(n):
+        o, c = lax.rem(n, members), lax.div(n, members)
         return {"client": h * members + flipped(o), "param": lax.rem(core + c, cores)}
 
-    def flipped(m):
-        return sum(b * lax.rem(lax.rem(lax.div(j, b), 2) + (m // b) % 2, 2) for b in bits)
-
-    full = members - 1
-    bits = [1 << b for b in range(full.bit_length())]
-    others = sorted(((o, c) for c in range(cores) for o in range(members) if o or c),
-                    key=lambda x: -bin(x[0]).count("1"))
+    def slot_of(n):
+        o, c = lax.rem(n, members), lax.div(n, members)
+        return lax.rem(core + c, cores) * members + flipped(o)
+
+    def each(low, high, do):
+        def body(n, carry):
+            do(n)
+            return carry
+
+        lax.fori_loop(low, high, body, 0)
+
+    everyone = cores * members
     barrier = pltpu.get_barrier_semaphore()
-    for o, c in others:
-        pl.semaphore_signal(barrier, inc=1, device_id=member(o, c), device_id_type=pl.DeviceIdType.MESH)
+    each(1, everyone, lambda n: pl.semaphore_signal(
+        barrier, inc=1, device_id=member(n), device_id_type=pl.DeviceIdType.MESH))
     if groups > 1:
         pl.semaphore_signal(barrier, inc=1, device_id={"client": partner}, device_id_type=pl.DeviceIdType.MESH)
     counts_in = pltpu.make_async_copy(cnt_hbm, cnt_ref, in_sem)
@@ -75,18 +86,10 @@
         sl = lanes(k)
         own.append(pltpu.make_async_copy(u_ref.at[:, :, j, :, sl], held.at[j, :, :, :, sl], own_sem.at[k]))
         own[-1].start()
-    pl.semaphore_wait(barrier, len(others) + (groups > 1))
-
-    masks = [full] + [m for low in range(members // 2 - 1, 0, -1) for m in (full - low, low)]
+    pl.semaphore_wait(barrier, everyone - 1 + (groups > 1))
 
     def peer(o):
-        m, index = masks[o - 1], 0
-        for b in bits:
-            flip = (m // b) % 2
-            if m != full:
-                flip = flip + lax.rem(core, 2) * (1 - 2 * flip)
-            index = index + b * lax.rem(lax.rem(lax.div(j, b), 2) + flip, 2)
-        return index
+        return flipped(o + lax.rem(core, 2) * (members - 2 * o))
 
     def count_copy(o, slot):
         return pltpu.make_async_remote_copy(
@@ -102,16 +105,14 @@
             device_id={"client": h * members + to}, device_id_type=pl.DeviceIdType.MESH)
 
     for k in range(chunks):
-        for o in range(1, members):
-            rows_copy(o, k, j).start()
+        each(1, members, lambda o, k=k: rows_copy(o, k, j).start())
         if k == 0:
             counts_in.wait()
             for c in range(nc):
                 row = jnp.full((1, LANES), cnt_ref[c], jnp.int32).astype(jnp.float32)
                 cnt_send[c:c + 1, :] = row
                 cnt_held[j, c:c + 1, :] = row
-            for o in range(1, members):
-                count_copy(o, j).start()
+            each(1, members, lambda o: count_copy(o, j).start())
 
     def part_copy(i, k):
         first = bounds[k] + (k > 0)
@@ -121,11 +122,11 @@
             send_sem=p_send.at[i, k], recv_sem=p_recv.at[i, k],
             device_id={"client": partner}, device_id_type=pl.DeviceIdType.MESH)
 
-    def dist_copy(i, n, o, c, slot):
+    def dist_copy(i, n, slot):
         return pltpu.make_async_remote_copy(
             src_ref=dist_send.at[i], dst_ref=dist_held.at[i, slot],
             send_sem=d_send.at[i, n], recv_sem=d_recv.at[i, n],
-            device_id=member(o, c), device_id_type=pl.DeviceIdType.MESH)
+            device_id=member(n), device_id_type=pl.DeviceIdType.MESH)
 
     def weights_now():
         w = [jnp.broadcast_to(weight[c:c + 1, :], (SUBLANES, LANES)) for c in range(clients)]
@@ -190,24 +191,25 @@
 
             return inverse, lax.fori_loop(bounds[k], bounds[k + 1], body, acc)
 
-        inverse, acc = None, tuple(jnp.zeros((SUBLANES, LANES), jnp.float32) for _ in range(clients))
         for k in range(chunks):
-            if i == 0:
+            @pl.when(i == 0)
+            def _(k=k):
                 own[k].wait()
-                for o in range(1, members):
-                    rows_copy(o, k, peer(o)).wait_recv()
+                each(1, members, lambda o: rows_copy(o, k, peer(o)).wait_recv())
+
             send_part(k)
-            if i == 0 and k > 0:
-                inverse, acc = add_distances(k - 1, inverse, acc)
-        if i == 1:
-            for o in range(1, members):
+
+        @pl.when(i == 1)
+        def _():
+            def sent(o):
                 count_copy(o, j).wait_send()
                 for k in range(chunks):
                     rows_copy(o, k, j).wait_send()
-        if i > 0:
-            for n, (o, c) in enumerate(others):
-                dist_copy(i - 1, n, o, c, rank).wait_send()
-        for k in range(chunks - 1 if i == 0 else 0, chunks):
+
+            each(1, members, sent)
+
+        inverse, acc = None, tuple(jnp.zeros((SUBLANES, LANES), jnp.float32) for _ in range(clients))
+        for k in range(chunks):
             inverse, acc = add_distances(k, inverse, acc)
         for c in range(clients):
             dist_rows[c:c + 1, :] = jnp.sum(acc[c], axis=0, keepdims=True)
@@ -218,10 +220,8 @@
         dist_send[i] = row
         dist_held[i, rank] = row
 
-        for n, (o, c) in enumerate(others):
-            dist_copy(i, n, o, c, rank).start()
-        for n, (o, c) in enumerate(others):
-            dist_copy(i, n, o, c, lax.rem(core + cores - c, cores) * members + flipped(o)).wait_recv()
+        each(1, everyone, lambda n: dist_copy(i, n, rank).start())
+        each(1, everyone, lambda n: dist_copy(i, n, slot_of(n)).wait_recv())
         row = dist_held[i, 0]
         for s in range(1, cores * members):
             row = row + dist_held[i, s]
@@ -230,12 +230,10 @@
         for c in range(clients):
             weight[c:c + 1, :] = cnt_held[c // nc, c % nc:c % nc + 1, :] / root[c:c + 1, :]
 
-    for o in range(1, members):
-        count_copy(o, peer(o)).wait_recv()
+    each(1, members, lambda o: count_copy(o, peer(o)).wait_recv())
     for c in range(clients):
         weight[c:c + 1, :] = cnt_held[c // nc, c % nc:c % nc + 1, :]
-    for i in range(ITERS):
-        iteration(i)
+    each(0, ITERS, iteration)
 
     w, total = weights_now()
     def final_copy(k):
@@ -261,8 +259,7 @@
         return carry
 
     lax.fori_loop(0, cols // LANES, body, 0)
-    for n, (o, c) in enumerate(others):
-        dist_copy(ITERS - 1, n, o, c, rank).wait_send()
+    each(1, everyone, lambda n: [dist_copy(i, n, rank).wait_send() for i in range(ITERS)])
     if groups > 1:
         for i in range(ITERS):
             for k in range(chunks):

time: 56.5 us -> 57.3 us (1.014)
  Pallas kernels: 54.6 us -> 55.4 us
    pallas_call x1, Pallas kernels: 54.6 us -> 55.4 us  [local(): pl.pallas_call(functools.partial(kernel, groups, members, cores, bounds,...]
where the time goes in v7:
time: 57.3 us; the launch traced here: 57.2 us
  Pallas kernels  55.4 us (97%)
  local copies, waits for them, and re-layouts  1.14 us (2%)
  between operations  0.64 us (1%)
    pallas_call x1, Pallas kernels, local(): pl.pallas_call(functools.partial(kernel, groups, members, cores, bounds,...  55.4 us

profile of v7, /device:TPU:0, one launch (start us, length us, event | category | flops | bytes accessed | tf_op | source)
XLA Modules:
  0.0 57.2 jit_solution(4247506166354932)
XLA Ops:
  0.6 55.4 %shard_map.41 = (f32[8,1792]{1,0:T(8,128)S(1)}, f32[2]{0:T(128)S(4)}) custom-call(f32[2,2,8,8,1792]{4,3,2,1,0:T(8,128)} %bitcast.1, s32[2]{0:T(128)} %cnt_hbm.1), custom_call_target="tpu_custom_call" | custom-call | flops 7340032 | bytes 3670016 | tf_op jit(solution)/shard_map/pallas_call | solution.py:306
  56.1 0.6 %copy.6 = f32[8,1792]{1,0:T(8,128)} copy(f32[8,1792]{1,0:T(8,128)S(1)} %get-tuple-element.2) | data formatting | bytes 114688
  56.7 0.5 copy.7

commit v8 on v4

--- a/solution.py
+++ b/solution.py
@@ -11,7 +11,8 @@
 LANES = 128
 SUBLANES = 8
 GROUPS = 2
-CHUNK_ENDS = (0.5, 0.79, 0.93, 1.0)
+CHUNK_ENDS = (0.57, 1.0)
+IN_FLIGHT = 2
 LAST_ENDS = (0.43, 1.0)
 
 smoothing = 1e-06
@@ -77,7 +78,7 @@
         own[-1].start()
     pl.semaphore_wait(barrier, len(others) + (groups > 1))
 
-    masks = [full] + [m for low in range(members // 2 - 1, 0, -1) for m in (full - low, low)]
+    masks = [m for low in range(1, members // 2) for m in (low, full - low)] + [full]
 
     def peer(o):
         m, index = masks[o - 1], 0
@@ -101,17 +102,20 @@
             send_sem=u_send.at[o, k], recv_sem=u_recv.at[o, k],
             device_id={"client": h * members + to}, device_id_type=pl.DeviceIdType.MESH)
 
-    for k in range(chunks):
-        for o in range(1, members):
-            rows_copy(o, k, j).start()
-        if k == 0:
+    sends = [(o, k) for k in range(chunks) for o in range(1, members)]
+    for n, (o, k) in enumerate(sends):
+        if n >= IN_FLIGHT:
+            before = sends[n - IN_FLIGHT]
+            rows_copy(*before, j).wait_send()
+        rows_copy(o, k, j).start()
+        if n == IN_FLIGHT - 1:
             counts_in.wait()
             for c in range(nc):
                 row = jnp.full((1, LANES), cnt_ref[c], jnp.int32).astype(jnp.float32)
                 cnt_send[c:c + 1, :] = row
                 cnt_held[j, c:c + 1, :] = row
-            for o in range(1, members):
-                count_copy(o, j).start()
+            for m in range(1, members):
+                count_copy(m, j).start()
 
     def part_copy(i, k):
         first = bounds[k] + (k > 0)
@@ -202,8 +206,8 @@
         if i == 1:
             for o in range(1, members):
                 count_copy(o, j).wait_send()
-                for k in range(chunks):
-                    rows_copy(o, k, j).wait_send()
+            for o, k in sends[-IN_FLIGHT:]:
+                rows_copy(o, k, j).wait_send()
         if i > 0:
             for n, (o, c) in enumerate(others):
                 dist_copy(i - 1, n, o, c, rank).wait_send()

time: 56.5 us -> 60.9 us (1.078)
  Pallas kernels: 54.6 us -> 59 us
    pallas_call x1, Pallas kernels: 54.6 us -> 59 us  [local(): pl.pallas_call(functools.partial(kernel, groups, members, cores, bounds,...]
where the time goes in v8:
time: 60.9 us; the launch traced here: 60.8 us
  Pallas kernels  59 us (97%)
  local copies, waits for them, and re-layouts  1.14 us (2%)
  between operations  0.64 us (1%)
    pallas_call x1, Pallas kernels, local(): pl.pallas_call(functools.partial(kernel, groups, members, cores, bounds,...  59 us

profile of v8, /device:TPU:0, one launch (start us, length us, event | category | flops | bytes accessed | tf_op | source)
XLA Modules:
  0.0 60.8 jit_solution(622220422165116942)
XLA Ops:
  0.6 59.0 %shard_map.41 = (f32[8,1792]{1,0:T(8,128)S(1)}, f32[2]{0:T(128)S(4)}) custom-call(f32[2,2,8,8,1792]{4,3,2,1,0:T(8,128)} %bitcast.1, s32[2]{0:T(128)} %cnt_hbm.1), custom_call_target="tpu_custom_call" | custom-call | flops 7340032 | bytes 3670016 | tf_op jit(solution)/shard_map/pallas_call | solution.py:313
  59.7 0.6 %copy.6 = f32[8,1792]{1,0:T(8,128)} copy(f32[8,1792]{1,0:T(8,128)S(1)} %get-tuple-element.2) | data formatting | bytes 114688
  60.3 0.5 copy.7

commit v9 on v4

--- a/solution.py
+++ b/solution.py
@@ -163,7 +163,7 @@
                     part[i, r, :, after(t)] = sum_tile(w, r, t)
                 return carry
 
-            lax.fori_loop(bounds[k], bounds[k + 1], body, 0)
+            lax.fori_loop(bounds[k], bounds[k + 1], body, 0, unroll=True)
             if groups > 1:
                 part_copy(i, k).start()
 
@@ -188,7 +188,7 @@
                         acc[c] = acc[c] + d * d
                 return tuple(acc)
 
-            return inverse, lax.fori_loop(bounds[k], bounds[k + 1], body, acc)
+            return inverse, lax.fori_loop(bounds[k], bounds[k + 1], body, acc, unroll=True)
 
         inverse, acc = None, tuple(jnp.zeros((SUBLANES, LANES), jnp.float32) for _ in range(clients))
         for k in range(chunks):
@@ -253,14 +253,14 @@
             return carry
 
         for k in range(len(ends) - 1):
-            lax.fori_loop(ends[k], ends[k + 1], body, 0)
+            lax.fori_loop(ends[k], ends[k + 1], body, 0, unroll=True)
             final_copy(k).start()
 
     def body(t, carry):
         med_ref[:, tile(t)] = sum_tile(w, h, t)
         return carry
 
-    lax.fori_loop(0, cols // LANES, body, 0)
+    lax.fori_loop(0, cols // LANES, body, 0, unroll=True)
     for n, (o, c) in enumerate(others):
         dist_copy(ITERS - 1, n, o, c, rank).wait_send()
     if groups > 1:
@@ -281,7 +281,7 @@
     for k in range(len(ends) - 1):
         if groups > 1 and k > 0:
             final_copy(k).wait_recv()
-        lax.fori_loop(ends[k], ends[k + 1], body, 0)
+        lax.fori_loop(ends[k], ends[k + 1], body, 0, unroll=True)
     for c in range(nc):
         share = (groups * clients) * weight[pl.ds(nc * j + c, 1), :] * inverse[0:1, :]
         share_ref[c] = share[0, 0]

time: 56.5 us -> 56.3 us (level)
  no operation moved by 1% of the time
where the time goes in v9:
time: 56.3 us; the launch traced here: 56.2 us
  Pallas kernels  54.4 us (97%)
  local copies, waits for them, and re-layouts  1.14 us (2%)
  between operations  0.64 us (1%)
    pallas_call x1, Pallas kernels, local(): pl.pallas_call(functools.partial(kernel, groups, members, cores, bounds,...  54.4 us
    unnamed x2, local copies, waits for them, and re-layouts  1.14 us

profile of v9, /device:TPU:0, one launch (start us, length us, event | category | flops | bytes accessed | tf_op | source)
XLA Modules:
  0.0 56.2 jit_solution(7463080305410868224)
XLA Ops:
  0.6 54.4 %shard_map.41 = (f32[8,1792]{1,0:T(8,128)S(1)}, f32[2]{0:T(128)S(4)}) custom-call(f32[2,2,8,8,1792]{4,3,2,1,0:T(8,128)} %bitcast.1, s32[2]{0:T(128)} %cnt_hbm.1), custom_call_target="tpu_custom_call" | custom-call | flops 7340032 | bytes 3670016 | tf_op jit(solution)/shard_map/pallas_call | solution.py:309
  55.0 0.6 %copy.6 = f32[8,1792]{1,0:T(8,128)} copy(f32[8,1792]{1,0:T(8,128)S(1)} %get-tuple-element.2) | data formatting | bytes 114688
  55.7 0.5 copy.7

commit v10 on v4

--- a/solution.py
+++ b/solution.py
@@ -10,8 +10,8 @@
 ITERS = 2
 LANES = 128
 SUBLANES = 8
-GROUPS = 2
-CHUNK_ENDS = (0.5, 0.79, 0.93, 1.0)
+GROUPS = 1
+CHUNK_ENDS = (0.5, 0.86, 1.0)
 LAST_ENDS = (0.43, 1.0)
 
 smoothing = 1e-06

time: 56.5 us -> 62.8 us (1.11)
  Pallas kernels: 54.6 us -> 60.8 us
    pallas_call x1, Pallas kernels: 54.6 us -> 60.8 us  [local(): pl.pallas_call(functools.partial(kernel, groups, members, cores, bounds,...]
where the time goes in v10:
time: 62.8 us; the launch traced here: 62.6 us
  Pallas kernels  60.8 us (97%)
  local copies, waits for them, and re-layouts  1.14 us (2%)
  between operations  0.64 us (1%)
    pallas_call x1, Pallas kernels, local(): pl.pallas_call(functools.partial(kernel, groups, members, cores, bounds,...  60.8 us

profile of v10, /device:TPU:0, one launch (start us, length us, event | category | flops | bytes accessed | tf_op | source)
XLA Modules:
  0.0 62.6 jit_solution(8458803647645414776)
XLA Ops:
  0.6 60.8 %shard_map.41 = (f32[8,1792]{1,0:T(8,128)S(1)}, f32[2]{0:T(128)S(4)}) custom-call(f32[2,1,16,8,1792]{4,3,2,1,0:T(8,128)} %bitcast.1, s32[2]{0:T(128)} %cnt_hbm.1), custom_call_target="tpu_custom_call" | custom-call | flops 7340032 | bytes 3670016 | tf_op jit(solution)/shard_map/pallas_call | solution.py:309
  61.5 0.6 copy.6
  62.1 0.5 copy.7
